TPU v7x, 32 devices: a whole 2x2x4 slice. The times are simulated.
32 devices in a mesh: blk: 4 (over x, core), wide: 8 (over z, y).
Axes of the slice: x: 2, y: 2, z: 4, core: 2. Of those that a mesh axis runs over, the one named last changes fastest.
Arguments:
- patch_keys: float32 [32, 196, 512], P(('blk', 'wide')), may hold values from -16 to 16
- patch_values: float32 [32, 196, 512], P(('blk', 'wide')), may hold values from -6 to 6
- caption_queries: float32 [32, 512], P(('blk', 'wide')), may hold values from -48 to 48
- positive: int32 [32, 32], P(('blk', 'wide')), may hold values 0 or 1
Outputs:
- grad_keys: float32 [32, 196, 512], P(('blk', 'wide'))
- grad_values: float32 [32, 196, 512], P(('blk', 'wide'))
- grad_queries: float32 [32, 512], P(('blk', 'wide'))
All inputs are finite; a program needn't handle non-finite values. No bound on the sum of `positive` on one device may be relied on, other than what follows from the above.
Results may differ from a plain program's by a relative error of at most 0.0005.
Values sent between devices are 32-bit elements; how exact they have to be, the bound alone decides.
A program may use at most 64 MiB of HBM per device.

v0:
```python
import jax
import jax.numpy as jnp
from jax import lax
from jax.sharding import PartitionSpec as P

HEADS = 8


epsilon = 1e-06
similarity_multiplier = 10.0
similarity_shift_term = -2.0


def passed_along(value, axis, steps):
    count = lax.axis_size(axis)
    pairs = [(source, (source + steps) % count) for source in range(count)]
    return lax.ppermute(value, axis, pairs)


def pair_loss(keys, values, queries, labels):
    images, patches, width = keys.shape
    row_count = queries.shape[0]
    head_dim = width // HEADS
    query_heads = queries.reshape(row_count, HEADS, head_dim)
    key_heads = keys.reshape(images, patches, HEADS, head_dim)
    value_heads = values.reshape(images, patches, HEADS, head_dim)
    scores = jnp.einsum(
        "chd,iphd->ichp", query_heads, key_heads, precision=lax.Precision.HIGHEST
    ) * head_dim ** (-0.5)
    row_max = lax.stop_gradient(jnp.max(scores, axis=3, keepdims=True))
    exponent = jnp.exp(scores - row_max)
    weights = exponent / jnp.sum(exponent, axis=3, keepdims=True)
    pooled = jnp.einsum(
        "ichp,iphd->ichd", weights, value_heads, precision=lax.Precision.HIGHEST
    ).reshape(images, row_count, width)
    matching_similarity = jnp.mean(pooled * queries[None], axis=2)
    summary_reciprocal_length = lax.rsqrt(jnp.mean(pooled * pooled, axis=2) + epsilon)
    probe_reciprocal_length = lax.rsqrt(jnp.mean(queries * queries, axis=1) + epsilon)
    matching_scaled_scores = (
        similarity_multiplier
        * matching_similarity
        * summary_reciprocal_length
        * probe_reciprocal_length[None]
        + similarity_shift_term
    )
    label_signs = 2.0 * labels.astype(jnp.float32) - 1.0
    return jnp.sum(jnp.logaddexp(0.0, -label_signs * matching_scaled_scores))


def pair_grads(keys, values, queries, labels):

    def loss_of(keys_in, values_in, input_queries):
        return pair_loss(keys_in, values_in, input_queries, labels)

    total, pull_back = jax.vjp(loss_of, keys, values, queries)
    return pull_back(jnp.ones_like(total))


def per_device(patch_keys, patch_values, caption_queries, positive):
    caption_group = lax.all_gather(caption_queries, "wide", axis=0, tiled=True)
    group_rows = caption_group.shape[0]
    cycle_size = lax.axis_size("blk")
    cycle_home = lax.axis_index("blk")
    key_zero = jnp.zeros_like(patch_keys)
    value_zero = jnp.zeros_like(patch_values)

    def cycle_turn(turn, carried):
        key_grad, value_grad, evaluate_objective, forward_acc, backward, backward_acc = carried
        source = (cycle_home - turn) % cycle_size
        labels_fwd = lax.dynamic_slice_in_dim(positive, source * group_rows, group_rows, 1)
        visiting = evaluate_objective
        key_part, value_part, query_part = pair_grads(
            patch_keys, patch_values, visiting, labels_fwd
        )
        forward_acc = forward_acc + query_part
        backward_acc = backward_acc + query_part[group_rows:]
        evaluate_objective, forward_acc = passed_along((evaluate_objective, forward_acc), "blk", 1)
        return (
            key_grad + key_part,
            value_grad + value_part,
            evaluate_objective,
            forward_acc,
            backward,
            backward_acc,
        )

    backward_start = caption_group[group_rows:]
    initial = (
        key_zero,
        value_zero,
        caption_group,
        jnp.zeros_like(caption_group),
        backward_start,
        jnp.zeros_like(backward_start),
    )
    grad_keys, grad_values, forward_end, forward_acc, backward_end, backward_acc = lax.fori_loop(
        0, cycle_size, cycle_turn, initial
    )
    group_grad = jnp.concatenate([forward_acc, backward_acc], 0)
    grad_queries = lax.psum_scatter(group_grad, "wide", scatter_dimension=0, tiled=True)
    return (grad_keys, grad_values, grad_queries)


def solution(mesh):
    in_specs = (
        P(("blk", "wide"), None, None),
        P(("blk", "wide"), None, None),
        P(("blk", "wide"), None),
        P(("blk", "wide"), None),
    )
    out_specs = (
        P(("blk", "wide"), None, None),
        P(("blk", "wide"), None, None),
        P(("blk", "wide"), None),
    )
    return jax.shard_map(
        per_device, mesh=mesh, in_specs=in_specs, out_specs=out_specs, check_vma=False
    )
```

profile of v0, /device:TPU:0, one launch (start us, length us, event | category | flops | bytes accessed | tf_op | source)
XLA Modules:
  0.0 97.5 jit_solution(4039821844923487244)
XLA Ops:
  0.6 1.3 %copy.28 = f32[1,196,512]{1,2,0:T(8,128)S(1)} copy(f32[1,196,512]{2,0,1:T(1,128)} %param.6) | data formatting | bytes 802816
  1.9 0.5 copy.29
  2.4 0.7 copy-done.2
  3.1 27.8 %all-gather = f32[8,1,512]{2,1,0:T(1,128)S(1)} all-gather(f32[1,1,512]{2,1,0:T(1,128)S(1)} %bitcast.249), channel_id=1, replica_groups=mesh['blk'=4,'wide'=8] {'wide'}, dimensions={0}, use_global_device_ids=true | all-gather | bytes 18432 | tf_op jit(solution)/shard_map/all_gather | solution.py:60
  30.9 0.6 copy-done.1
  31.5 25.8 %while.23 = (s32[]{:T(128)}, f32[1,196,512]{1,2,0:T(8,128)S(1)}, f32[1,196,512]{1,2,0:T(8,128)S(1)}, f32[8,512]{1,0:T(8,128)S(1)}, f32[8,512]{1,0:T(8,128)S(1)},...) while((s32[]{:T(128)}, f32[1,196,512]{1,2,0:T(8,128)S(1)}, ...), condition=%wide.region_7.8_spmd.clone, body=%wide.region_0.7_spmd.clone.sunk | while | flops 58545992 | bytes 5947378 | solution.py:96
  31.6 0.5 bitcast_reduce_fusion.2
  32.1 0.2 fusion.65
  32.3 0.7 multiply_reduce_fusion.5
  33.5 0.4 fusion.69
  34.0 0.6 convolution_bitcast_fusion.3
  34.7 1.6 %collective-permute-start.1 = (f32[8,512]{1,0:T(8,128)S(1)}, f32[8,512]{1,0:T(8,128)S(1)}, u32[]{:S(2)}, u32[]{:S(2)}) collective-permute-start(f32[8,512]{1,0:T(8,128)S(1)} %fusion.71), channel_id=1, source_target_pairs={{0,8},{8,16},{16,24},{24,0},{1,9},{9,17},{17,25},{25,1},{2,10},{10... | collective-permute-start | bytes 49160 | tf_op jit(solution)/shard_map/while/body/eval_jaxpr/ppermute | solution.py:17
  36.3 0.7 fusion.70
  37.0 0.7 fusion.68
  37.8 0.3 bitcast_add_fusion.3
  38.3 0.5 bitcast_reduce_fusion.2
  38.8 0.2 fusion.65
  39.0 0.7 multiply_reduce_fusion.5
  40.2 0.4 fusion.69
  40.6 0.6 convolution_bitcast_fusion.3
  41.4 1.3 %collective-permute-start.1 = (f32[8,512]{1,0:T(8,128)S(1)}, f32[8,512]{1,0:T(8,128)S(1)}, u32[]{:S(2)}, u32[]{:S(2)}) collective-permute-start(f32[8,512]{1,0:T(8,128)S(1)} %fusion.71), channel_id=1, source_target_pairs={{0,8},{8,16},{16,24},{24,0},{1,9},{9,17},{17,25},{25,1},{2,10},{10... | collective-permute-start | bytes 49160 | tf_op jit(solution)/shard_map/while/body/eval_jaxpr/ppermute | solution.py:17
  42.7 0.7 fusion.70
  43.4 0.7 fusion.68
  44.1 0.3 bitcast_add_fusion.3
  44.7 0.5 bitcast_reduce_fusion.2
  45.2 0.2 fusion.65
  45.3 0.7 multiply_reduce_fusion.5
  46.6 0.4 fusion.69
  47.0 0.6 convolution_bitcast_fusion.3
  47.8 1.3 %collective-permute-start.1 = (f32[8,512]{1,0:T(8,128)S(1)}, f32[8,512]{1,0:T(8,128)S(1)}, u32[]{:S(2)}, u32[]{:S(2)}) collective-permute-start(f32[8,512]{1,0:T(8,128)S(1)} %fusion.71), channel_id=1, source_target_pairs={{0,8},{8,16},{16,24},{24,0},{1,9},{9,17},{17,25},{25,1},{2,10},{10... | collective-permute-start | bytes 49160 | tf_op jit(solution)/shard_map/while/body/eval_jaxpr/ppermute | solution.py:17
  49.1 0.7 fusion.70
  49.8 0.7 fusion.68
  50.5 0.3 bitcast_add_fusion.3
  51.1 0.5 bitcast_reduce_fusion.2
  51.5 0.2 fusion.65
  51.7 0.7 multiply_reduce_fusion.5
  52.9 0.4 fusion.69
  53.4 0.6 convolution_bitcast_fusion.3
  54.2 1.3 %collective-permute-start.1 = (f32[8,512]{1,0:T(8,128)S(1)}, f32[8,512]{1,0:T(8,128)S(1)}, u32[]{:S(2)}, u32[]{:S(2)}) collective-permute-start(f32[8,512]{1,0:T(8,128)S(1)} %fusion.71), channel_id=1, source_target_pairs={{0,8},{8,16},{16,24},{24,0},{1,9},{9,17},{17,25},{25,1},{2,10},{10... | collective-permute-start | bytes 49160 | tf_op jit(solution)/shard_map/while/body/eval_jaxpr/ppermute | solution.py:17
  55.4 0.7 fusion.70
  56.1 0.7 fusion.68
  56.9 0.3 bitcast_add_fusion.3
  57.3 1.0 %copy.30 = f32[1,196,512]{2,0,1:T(1,128)} copy(f32[1,196,512]{1,2,0:T(8,128)S(1)} %get-tuple-element.324) | data formatting | bytes 802816
  58.3 1.0 %copy.31 = f32[1,196,512]{2,0,1:T(1,128)} copy(f32[1,196,512]{1,2,0:T(8,128)S(1)} %get-tuple-element.325) | data formatting | bytes 802816
  59.3 35.6 %all-reduce = f32[8,512]{1,0:T(8,128)S(1)} all-reduce(f32[8,512]{1,0:T(8,128)S(1)} %get-tuple-element.260), channel_id=2, replica_groups=mesh['blk'=4,'wide'=8] {'wide'}, use_global_device_ids=true, to_apply=%region_8.9.clone | all-reduce | flops 4096 | bytes 32768
  94.9 0.7 copy-done.3
  95.6 0.7 dynamic-slice
  96.2 1.3 %constant_dynamic-slice_fusion = f32[1,512]{1,0:T(1,128)} fusion(f32[8,512]{1,0:T(8,128)S(1)} %all-reduce, u32[]{:T(128)} %bitcast.36), kind=kLoop, calls=%fused_computation.63 | loop fusion | bytes 4100
  (77 shorter events, 3.5 us)
Async XLA Ops:
  0.6 1.3 %copy-start = (f32[1,196,512]{2,0,1:T(1,128)S(1)}, f32[1,196,512]{2,0,1:T(1,128)}, u32[]{:S(2)}) copy-start(f32[1,196,512]{2,0,1:T(1,128)} %param.7) | copy-start | bytes 1204228
  2.4 0.7 copy-start.2
  30.9 0.7 copy-start.1
  31.5 6.6 %collective-permute-start = (f32[8,512]{1,0:T(8,128)S(1)}, f32[8,512]{1,0:T(8,128)S(1)}, u32[]{:S(2)}, u32[]{:S(2)}) collective-permute-start(f32[8,512]{1,0:T(8,128)S(1)} %copy.71), channel_id=1, source_target_pairs={{0,8},{8,16},{16,24},{24,0},{1,9},{9,17},{17,25},{25,1},{2,10},{10... | collective-permute-start | bytes 49160 | tf_op jit(solution)/shard_map/while/body/eval_jaxpr/ppermute | solution.py:17
  34.7 3.4 %collective-permute-start.1 = (f32[8,512]{1,0:T(8,128)S(1)}, f32[8,512]{1,0:T(8,128)S(1)}, u32[]{:S(2)}, u32[]{:S(2)}) collective-permute-start(f32[8,512]{1,0:T(8,128)S(1)} %fusion.71), channel_id=1, source_target_pairs={{0,8},{8,16},{16,24},{24,0},{1,9},{9,17},{17,25},{25,1},{2,10},{10... | collective-permute-start | bytes 49160 | tf_op jit(solution)/shard_map/while/body/eval_jaxpr/ppermute | solution.py:17
  38.1 6.4 %collective-permute-start = (f32[8,512]{1,0:T(8,128)S(1)}, f32[8,512]{1,0:T(8,128)S(1)}, u32[]{:S(2)}, u32[]{:S(2)}) collective-permute-start(f32[8,512]{1,0:T(8,128)S(1)} %copy.71), channel_id=1, source_target_pairs={{0,8},{8,16},{16,24},{24,0},{1,9},{9,17},{17,25},{25,1},{2,10},{10... | collective-permute-start | bytes 49160 | tf_op jit(solution)/shard_map/while/body/eval_jaxpr/ppermute | solution.py:17
  41.4 3.2 %collective-permute-start.1 = (f32[8,512]{1,0:T(8,128)S(1)}, f32[8,512]{1,0:T(8,128)S(1)}, u32[]{:S(2)}, u32[]{:S(2)}) collective-permute-start(f32[8,512]{1,0:T(8,128)S(1)} %fusion.71), channel_id=1, source_target_pairs={{0,8},{8,16},{16,24},{24,0},{1,9},{9,17},{17,25},{25,1},{2,10},{10... | collective-permute-start | bytes 49160 | tf_op jit(solution)/shard_map/while/body/eval_jaxpr/ppermute | solution.py:17
  44.6 6.4 %collective-permute-start = (f32[8,512]{1,0:T(8,128)S(1)}, f32[8,512]{1,0:T(8,128)S(1)}, u32[]{:S(2)}, u32[]{:S(2)}) collective-permute-start(f32[8,512]{1,0:T(8,128)S(1)} %copy.71), channel_id=1, source_target_pairs={{0,8},{8,16},{16,24},{24,0},{1,9},{9,17},{17,25},{25,1},{2,10},{10... | collective-permute-start | bytes 49160 | tf_op jit(solution)/shard_map/while/body/eval_jaxpr/ppermute | solution.py:17
  47.8 3.2 %collective-permute-start.1 = (f32[8,512]{1,0:T(8,128)S(1)}, f32[8,512]{1,0:T(8,128)S(1)}, u32[]{:S(2)}, u32[]{:S(2)}) collective-permute-start(f32[8,512]{1,0:T(8,128)S(1)} %fusion.71), channel_id=1, source_target_pairs={{0,8},{8,16},{16,24},{24,0},{1,9},{9,17},{17,25},{25,1},{2,10},{10... | collective-permute-start | bytes 49160 | tf_op jit(solution)/shard_map/while/body/eval_jaxpr/ppermute | solution.py:17
  51.0 6.4 %collective-permute-start = (f32[8,512]{1,0:T(8,128)S(1)}, f32[8,512]{1,0:T(8,128)S(1)}, u32[]{:S(2)}, u32[]{:S(2)}) collective-permute-start(f32[8,512]{1,0:T(8,128)S(1)} %copy.71), channel_id=1, source_target_pairs={{0,8},{8,16},{16,24},{24,0},{1,9},{9,17},{17,25},{25,1},{2,10},{10... | collective-permute-start | bytes 49160 | tf_op jit(solution)/shard_map/while/body/eval_jaxpr/ppermute | solution.py:17
  54.2 3.2 %collective-permute-start.1 = (f32[8,512]{1,0:T(8,128)S(1)}, f32[8,512]{1,0:T(8,128)S(1)}, u32[]{:S(2)}, u32[]{:S(2)}) collective-permute-start(f32[8,512]{1,0:T(8,128)S(1)} %fusion.71), channel_id=1, source_target_pairs={{0,8},{8,16},{16,24},{24,0},{1,9},{9,17},{17,25},{25,1},{2,10},{10... | collective-permute-start | bytes 49160 | tf_op jit(solution)/shard_map/while/body/eval_jaxpr/ppermute | solution.py:17
  94.9 0.7 copy-start.3
where the time goes:
time: 97.7 us; the launch traced here: 97.5 us
  blocking collectives  63.3 us (65%)
  matrix products  14.4 us (15%)
  local copies, waits for them, and re-layouts  8.96 us (9%)
  starting transfers between devices  5.48 us (6%)
  other arithmetic  3.75 us (4%)
    unnamed x1, blocking collectives  35.6 us
    all_gather x1, blocking collectives, per_device(): caption_group = lax.all_gather(caption_queries, 'wide', axis=0, tiled=True)  27.8 us
    unnamed x15, local copies, waits for them, and re-layouts  7.65 us
    dot_general x12, matrix products, pair_loss(): jnp.einsum('ichp,iphd->ichd', weights, value_heads, precision=lax.Precisi...  7.36 us
    dot_general x12, matrix products, pair_loss(): jnp.einsum('chd,iphd->ichp', query_heads, key_heads, precision=lax.Precis...  7.08 us
    ppermute x8, starting transfers between devices, passed_along(): return lax.ppermute(value, axis, pairs)  5.48 us
  transfers between devices with their start and end apart: 8, of which 3 were waited for; matrix products, arithmetic and copies ran while one was open for 20% of the time, Pallas kernels for 0%

commit v1 on v0

v1 whole, which is shorter than its diff:
```python
import functools

import jax
import jax.numpy as jnp
from jax import lax
from jax.experimental import pallas as pl
from jax.experimental.pallas import tpu as pltpu
from jax.sharding import PartitionSpec as P

HEADS = 8
GROUP = 256
LANES = 128

epsilon = 1e-06
similarity_multiplier = 10.0
similarity_shift_term = -2.0

MESH = pl.DeviceIdType.MESH
F32 = jnp.float32
BF16 = jnp.bfloat16


def split(x):
    high = x.astype(BF16)
    return high, (x - high.astype(F32)).astype(BF16)


def dot3(a, b, dims):
    def one(x, y):
        return lax.dot_general(x, y, (dims, ((), ())), preferred_element_type=F32)

    return one(a[0], b[0]) + (one(a[0], b[1]) + one(a[1], b[0]))


NN = ((1,), (0,))
NT = ((1,), (1,))
TN = ((0,), (0,))


def remote(src, dst, send, recv, where):
    return pltpu.make_async_remote_copy(
        src_ref=src, dst_ref=dst, send_sem=send, recv_sem=recv,
        device_id=where, device_id_type=MESH,
    )


def kernel(
    nblk, nwide, block,
    k_hbm, v_hbm, q_ref, pos_ref,
    dk_hbm, dv_hbm, dq_ref,
    k_in, v_in, khi, klo, vhi, vlo, dk_buf, dv_buf,
    gath, part, land1, acc, land2,
    load_sem, store_sem,
    g1s, g1r, g2s, g2r, r1s, r1r, r2s, r2r,
):
    padded, width = khi.shape
    pieces = width // LANES
    patches = k_hbm.shape[0] // pieces
    rows = gath.shape[0]
    groups = width // GROUP
    head_dim = width // HEADS
    per_group = GROUP // head_dim
    scale = head_dim ** (-0.5)
    me_b = lax.axis_index("blk")
    me_w = lax.axis_index("wide")
    me = me_b * nwide + me_w

    k_load = pltpu.make_async_copy(k_hbm, k_in, load_sem.at[0])
    v_load = pltpu.make_async_copy(v_hbm, v_in, load_sem.at[1])
    k_load.start()
    v_load.start()

    wide_peers = [lax.rem(me_w + s, nwide) for s in range(1, nwide)]
    blk_peers = [lax.rem(me_b + s, nblk) for s in range(1, nblk)]

    barrier = pltpu.get_barrier_semaphore()
    for w in wide_peers:
        pl.semaphore_signal(barrier, inc=1, device_id=(me_b, w), device_id_type=MESH)
    for b in blk_peers:
        pl.semaphore_signal(barrier, inc=1, device_id=(b, me_w), device_id_type=MESH)

    gath[pl.ds(me, 1), :] = q_ref[...]
    pl.semaphore_wait(barrier, nblk + nwide - 2)

    mine = gath.at[pl.ds(me, 1)]
    sends1 = []
    for s, w in enumerate(wide_peers):
        copy = remote(q_ref, mine, g1s.at[s], g1r.at[s], (me_b, w))
        copy.start()
        sends1.append(copy)

    def prepare(load, raw, high, low):
        load.wait()
        if padded > patches:
            tail = patches // 16 * 16
            high[tail:, :] = jnp.zeros((padded - tail, width), BF16)
            low[tail:, :] = jnp.zeros((padded - tail, width), BF16)
        for g in range(pieces):
            h, l = split(raw[pl.ds(g, patches, stride=pieces), :])
            high[:patches, g * LANES:(g + 1) * LANES] = h
            low[:patches, g * LANES:(g + 1) * LANES] = l

    prepare(k_load, k_in, khi, klo)

    for copy in sends1:
        copy.wait_recv()
    own = gath.at[pl.ds(pl.multiple_of(me_b * nwide, nwide), nwide)]
    sends2 = []
    for s, b in enumerate(blk_peers):
        copy = remote(own, own, g2s.at[s], g2r.at[s], (b, me_w))
        copy.start()
        sends2.append(copy)

    prepare(v_load, v_in, vhi, vlo)

    for copy in sends2:
        copy.wait_recv()

    stacked = per_group * block
    row = lax.broadcasted_iota(jnp.int32, (stacked, GROUP), 0) // block
    col = lax.broadcasted_iota(jnp.int32, (stacked, GROUP), 1) // head_dim
    on_head = row == col
    valid = lax.broadcasted_iota(jnp.int32, (stacked, padded), 1) < patches

    def spread(x):
        return jnp.where(on_head, jnp.concatenate([x] * per_group, axis=0), 0.0)

    def gathered(x):
        x = jnp.where(on_head, x, 0.0)
        return sum(x[h * block:(h + 1) * block] for h in range(per_group))

    def cut(ref, j):
        return ref[:, j * GROUP:(j + 1) * GROUP]

    def chunk(at):
        q = gath[pl.ds(at, block), :]
        pos = pos_ref[at // block]
        eye = lax.broadcasted_iota(jnp.int32, (block, block), 0) == lax.broadcasted_iota(
            jnp.int32, (block, block), 1
        )
        label = jnp.sum(jnp.where(eye, pos.astype(F32), 0.0), axis=1, keepdims=True)
        sign = 2.0 * label - 1.0
        q_mean = jnp.mean(q * q, axis=1, keepdims=True)
        qg = [q[:, j * GROUP:(j + 1) * GROUP] for j in range(groups)]
        qbd = [split(spread(x * scale)) for x in qg]

        e, e2, rinv, pooled = [], [], [], []
        for j in range(groups):
            s = dot3(qbd[j], (cut(khi, j), cut(klo, j)), NT)
            s = jnp.where(valid, s, -3e38)
            x = jnp.exp(s - jnp.max(s, axis=1, keepdims=True))
            e.append(x)
            e2.append(split(x))
            rinv.append(1.0 / jnp.sum(x, axis=1, keepdims=True))
            y = dot3(e2[j], (cut(vhi, j), cut(vlo, j)), NN)
            pooled.append(gathered(y * rinv[j]))

        a = sum(jnp.sum(p * x, axis=1, keepdims=True) for p, x in zip(pooled, qg)) / width
        b = sum(jnp.sum(p * p, axis=1, keepdims=True) for p in pooled) / width
        r = lax.rsqrt(b + epsilon)
        u = lax.rsqrt(q_mean + epsilon)
        logit = similarity_multiplier * a * r * u + similarity_shift_term
        g = -sign / (1.0 + jnp.exp(sign * logit))
        t = g * (similarity_multiplier / width) * r * u
        ar = t * a * r * r
        au = t * a * u * u

        ds2, dpbd = [], []
        for j in range(groups):
            dp = t * qg[j] - ar * pooled[j]
            full = spread(dp) * rinv[j]
            pd = jnp.concatenate([pooled[j]] * per_group, axis=0)
            rs = jnp.sum(full * pd, axis=1, keepdims=True)
            dpbd.append(split(full))
            dw = dot3(dpbd[j], (cut(vhi, j), cut(vlo, j)), NT)
            ds = e[j] * (dw - rs)
            ds2.append(split(ds))
            dq = gathered(dot3(ds2[j], (cut(khi, j), cut(klo, j)), NN)) * scale
            part[pl.ds(at, block), j * GROUP:(j + 1) * GROUP] = dq + (t * pooled[j] - au * qg[j])
        return qbd, e2, ds2, dpbd

    def finish(state, add):
        qbd, e2, ds2, dpbd = state
        for j in range(groups):
            dk = dot3(ds2[j], qbd[j], TN)[:patches]
            dv = dot3(e2[j], dpbd[j], TN)[:patches]
            for i in range(GROUP // LANES):
                lines = pl.ds(j * (GROUP // LANES) + i, patches, stride=pieces)
                lanes = slice(i * LANES, (i + 1) * LANES)
                if add:
                    dk_buf[lines, :] += dk[:, lanes]
                    dv_buf[lines, :] += dv[:, lanes]
                else:
                    dk_buf[lines, :] = dk[:, lanes]
                    dv_buf[lines, :] = dv[:, lanes]

    one = rows == block
    if one:
        state = chunk(0)
    else:
        dk_buf[...] = jnp.zeros_like(dk_buf)
        dv_buf[...] = jnp.zeros_like(dv_buf)

        def step(i, carry):
            finish(chunk(pl.multiple_of(i * block, block)), True)
            return carry

        lax.fori_loop(0, rows // block, step, 0)

    sends3 = []
    for s, b in enumerate(blk_peers):
        copy = remote(
            part.at[pl.ds(pl.multiple_of(b * nwide, nwide), nwide)],
            land1.at[s], r1s.at[s], r1r.at[s], (b, me_w),
        )
        copy.start()
        sends3.append(copy)

    if one:
        finish(state, False)
    dk_store = pltpu.make_async_copy(dk_buf, dk_hbm, store_sem.at[0])
    dv_store = pltpu.make_async_copy(dv_buf, dv_hbm, store_sem.at[1])
    dk_store.start()
    dv_store.start()

    total = part[pl.ds(pl.multiple_of(me_b * nwide, nwide), nwide), :]
    for s, copy in enumerate(sends3):
        copy.wait_recv()
        total = total + land1[s]
    acc[...] = total

    sends4 = []
    for s, w in enumerate(wide_peers):
        copy = remote(
            acc.at[pl.ds(w, 1)], land2.at[pl.ds(s, 1)], r2s.at[s], r2r.at[s], (me_b, w)
        )
        copy.start()
        sends4.append(copy)
    final = acc[pl.ds(me_w, 1), :]
    for copy in sends4:
        copy.wait_recv()
    final = final + jnp.sum(land2[:nwide - 1, :], axis=0, keepdims=True)
    dq_ref[...] = final

    for copy in sends1 + sends2 + sends3 + sends4:
        copy.wait_send()
    dk_store.wait()
    dv_store.wait()


def per_device(nblk, nwide, patch_keys, patch_values, caption_queries, positive):
    _, patches, width = patch_keys.shape
    rows = positive.shape[1]
    padded = -(-patches // LANES) * LANES
    block = 32 if rows % 32 == 0 else rows
    lines = patches * width // LANES
    flat = (lines, LANES)
    any_space = pl.BlockSpec(memory_space=pltpu.HBM)
    vmem = pl.BlockSpec(memory_space=pltpu.VMEM)
    dma = pltpu.SemaphoreType.DMA
    dk, dv, dq = pl.pallas_call(
        functools.partial(kernel, nblk, nwide, block),
        out_shape=(
            jax.ShapeDtypeStruct(flat, F32),
            jax.ShapeDtypeStruct(flat, F32),
            jax.ShapeDtypeStruct(caption_queries.shape, F32),
        ),
        in_specs=[any_space, any_space, vmem, vmem],
        out_specs=(any_space, any_space, vmem),
        scratch_shapes=[
            pltpu.VMEM(flat, F32),
            pltpu.VMEM(flat, F32),
            pltpu.VMEM((padded, width), BF16),
            pltpu.VMEM((padded, width), BF16),
            pltpu.VMEM((padded, width), BF16),
            pltpu.VMEM((padded, width), BF16),
            pltpu.VMEM(flat, F32),
            pltpu.VMEM(flat, F32),
            pltpu.VMEM((rows, width), F32),
            pltpu.VMEM((rows, width), F32),
            pltpu.VMEM((nblk - 1, nwide, width), F32),
            pltpu.VMEM((nwide, width), F32),
            pltpu.VMEM((nwide, width), F32),
            dma((2,)),
            dma((2,)),
            dma((nwide - 1,)), dma((nwide - 1,)),
            dma((nblk - 1,)), dma((nblk - 1,)),
            dma((nblk - 1,)), dma((nblk - 1,)),
            dma((nwide - 1,)), dma((nwide - 1,)),
        ],
        compiler_params=pltpu.CompilerParams(
            collective_id=0, has_side_effects=True, vmem_limit_bytes=60 * 1024 * 1024
        ),
        cost_estimate=pl.CostEstimate(
            flops=6 * 2 * 3 * rows * patches * width,
            bytes_accessed=4 * 4 * patches * width,
            transcendentals=rows * HEADS * patches,
        ),
    )(
        patch_keys.reshape(flat),
        patch_values.reshape(flat),
        caption_queries,
        positive.reshape(rows // block, 1, block),
    )
    return dk.reshape(patch_keys.shape), dv.reshape(patch_values.shape), dq


def solution(mesh):
    in_specs = (
        P(("blk", "wide"), None, None),
        P(("blk", "wide"), None, None),
        P(("blk", "wide"), None),
        P(("blk", "wide"), None),
    )
    out_specs = (
        P(("blk", "wide"), None, None),
        P(("blk", "wide"), None, None),
        P(("blk", "wide"), None),
    )
    body = functools.partial(per_device, mesh.shape["blk"], mesh.shape["wide"])
    return jax.shard_map(body, mesh=mesh, in_specs=in_specs, out_specs=out_specs, check_vma=False)
```

time: 97.7 us -> 27.5 us (0.28)
  blocking collectives: 63.3 us -> 0 us
  Pallas kernels: 0 us -> 23.3 us
  matrix products: 14.4 us -> 0 us
  local copies, waits for them, and re-layouts: 8.96 us -> 3.41 us
  starting transfers between devices: 5.48 us -> 0 us
  other arithmetic: 3.75 us -> 0 us
    unnamed x1 -> x0, blocking collectives: 35.6 us -> none
    all_gather x1 -> x0, blocking collectives: 27.8 us -> none  [per_device(): caption_group = lax.all_gather(caption_queries, 'wide', axis=0, tiled=True)]
    pallas_call x0 -> x1, Pallas kernels: none -> 23.3 us  [per_device(): pl.pallas_call(functools.partial(kernel, nblk, nwide, block), out_shape=(...]
    dot_general x24 -> x0, matrix products: 14.4 us -> none  [the longest x12 7.36 us: pair_loss(): jnp.einsum('ichp,iphd->ichd', weights, value_heads, precision=lax.Precisi...]
    ppermute x8 -> x0, starting transfers between devices: 5.48 us -> none  [passed_along(): return lax.ppermute(value, axis, pairs)]
    unnamed x15 -> x7, local copies, waits for them, and re-layouts: 7.65 us -> 3.41 us
    add x8 -> x0, other arithmetic: 1.66 us -> none  [the longest x4 1.35 us: cycle_turn(): value_grad + value_part]
    reduce_sum x8 -> x0, other arithmetic: 1.26 us -> none  [the longest x4 0.66 us: pair_loss(): weights = exponent / jnp.sum(exponent, axis=3, keepdims=True)]
  transfers between devices with their start and end apart: 8 -> 0, of which waited for: 3 -> 0; matrix products, arithmetic and copies ran while one was open for 20% -> 0% of each run, Pallas kernels for 0% -> 0%
where the time goes in v1:
time: 27.5 us; the launch traced here: 27.3 us
  Pallas kernels  23.3 us (85%)
  local copies, waits for them, and re-layouts  3.41 us (12%)
  between operations  0.65 us (2%)
    pallas_call x1, Pallas kernels, per_device(): pl.pallas_call(functools.partial(kernel, nblk, nwide, block), out_shape=(...  23.3 us
    unnamed x7, local copies, waits for them, and re-layouts  3.41 us

profile of v1, /device:TPU:0, one launch (start us, length us, event | category | flops | bytes accessed | tf_op | source)
XLA Modules:
  0.0 27.3 jit_solution(5652563034033564439)
XLA Ops:
  0.6 23.3 %shard_map.67 = (f32[784,128]{1,0:T(8,128)}, f32[784,128]{1,0:T(8,128)}, f32[1,512]{1,0:T(1,128)}) custom-call(f32[784,128]{1,0:T(8,128)} %bitcast.5, f32[784,128]{1,0:T(8,128)} %bitcast.6, f32[1,512]{1,0:T(1,128)} %q_ref.1, s32[1,1,32]{2,1,0:T(1,128)} %bitcast.9), custom_call_target="tpu_custom_call" | custom-call | flops 115605504 | bytes 1605632 | tf_op jit(solution)/shard_map/pallas_call | solution.py:261
  23.9 0.0 copy-start
  23.9 2.1 %copy.14 = f32[1,196,512]{2,0,1:T(1,128)} copy(f32[1,196,512]{2,0,1:T(1,128)} %bitcast.8) | data formatting | bytes 802816
  26.0 0.0 copy-done
  26.0 0.0 copy-start.1
  26.0 0.7 %copy.15 = f32[1,196,512]{2,0,1:T(1,128)} copy(f32[1,196,512]{2,0,1:T(1,128)S(1)} %bitcast.7) | data formatting | bytes 802816
  26.8 0.0 copy-done.1
  26.8 0.6 %copy.16 = f32[1,512]{1,0:T(1,128)} copy(f32[1,512]{1,0:T(1,128)S(1)} %copy-done.1) | data formatting | bytes 4096
Async XLA Ops:
  23.9 2.1 %copy-start = (f32[784,128]{1,0:T(8,128)S(1)}, f32[784,128]{1,0:T(8,128)}, u32[]{:S(2)}) copy-start(f32[784,128]{1,0:T(8,128)} %get-tuple-element.7) | copy-start | bytes 1204228
  26.0 0.8 %copy-start.1 = (f32[1,512]{1,0:T(1,128)S(1)}, f32[1,512]{1,0:T(1,128)}, u32[]{:S(2)}) copy-start(f32[1,512]{1,0:T(1,128)} %get-tuple-element.20) | copy-start | bytes 6148

commit v2 on v1

--- a/solution.py
+++ b/solution.py
@@ -37,21 +37,27 @@
 TN = ((0,), (0,))
 
 
-def remote(src, dst, send, recv, where):
-    return pltpu.make_async_remote_copy(
-        src_ref=src, dst_ref=dst, send_sem=send, recv_sem=recv,
-        device_id=where, device_id_type=MESH,
-    )
+def each(count, body):
+    if count <= 64:
+        for i in range(count):
+            body(i)
+    else:
+        lax.fori_loop(0, count, lambda i, carry: (body(i), carry)[1], 0)
+
+
+def offsets(slot, nblk, nwide):
+    turn = slot // nblk
+    half = (turn + 1) // 2
+    odd = turn % 2
+    return slot % nblk, odd * half + (1 - odd) * ((nwide - half) % nwide)
 
 
 def kernel(
     nblk, nwide, block,
     k_hbm, v_hbm, q_ref, pos_ref,
-    dk_hbm, dv_hbm, dq_ref,
-    k_in, v_in, khi, klo, vhi, vlo, dk_buf, dv_buf,
-    gath, part, land1, acc, land2,
-    load_sem, store_sem,
-    g1s, g1r, g2s, g2r, r1s, r1r, r2s, r2r,
+    dk_buf, dv_buf, land,
+    k_in, v_in, khi, klo, vhi, vlo, gath, part,
+    load_sem, store_sem, gs, gr, rs_sem, rr,
 ):
     padded, width = khi.shape
     pieces = width // LANES
@@ -63,31 +69,43 @@
     scale = head_dim ** (-0.5)
     me_b = lax.axis_index("blk")
     me_w = lax.axis_index("wide")
-    me = me_b * nwide + me_w
 
     k_load = pltpu.make_async_copy(k_hbm, k_in, load_sem.at[0])
     v_load = pltpu.make_async_copy(v_hbm, v_in, load_sem.at[1])
     k_load.start()
     v_load.start()
 
-    wide_peers = [lax.rem(me_w + s, nwide) for s in range(1, nwide)]
-    blk_peers = [lax.rem(me_b + s, nblk) for s in range(1, nblk)]
+    def ahead(slot):
+        a, b = offsets(slot, nblk, nwide)
+        return lax.rem(me_b + a, nblk), lax.rem(me_w + b, nwide)
+
+    def behind(slot):
+        a, b = offsets(slot, nblk, nwide)
+        return lax.rem(me_b + (nblk - a), nblk), lax.rem(me_w + (nwide - b), nwide)
+
+    def gather_copy(i):
+        slot = rows - 1 - i
+        return pltpu.make_async_remote_copy(
+            src_ref=q_ref, dst_ref=gath.at[pl.ds(slot, 1)],
+            send_sem=gs.at[i], recv_sem=gr.at[i],
+            device_id=ahead(slot), device_id_type=MESH,
+        )
+
+    def scatter_copy(i):
+        slot = rows - 1 - i
+        return pltpu.make_async_remote_copy(
+            src_ref=part.at[pl.ds(slot, 1)], dst_ref=land.at[pl.ds(slot, 1)],
+            send_sem=rs_sem.at[i], recv_sem=rr.at[i],
+            device_id=behind(slot), device_id_type=MESH,
+        )
 
     barrier = pltpu.get_barrier_semaphore()
-    for w in wide_peers:
-        pl.semaphore_signal(barrier, inc=1, device_id=(me_b, w), device_id_type=MESH)
-    for b in blk_peers:
-        pl.semaphore_signal(barrier, inc=1, device_id=(b, me_w), device_id_type=MESH)
-
-    gath[pl.ds(me, 1), :] = q_ref[...]
-    pl.semaphore_wait(barrier, nblk + nwide - 2)
-
-    mine = gath.at[pl.ds(me, 1)]
-    sends1 = []
-    for s, w in enumerate(wide_peers):
-        copy = remote(q_ref, mine, g1s.at[s], g1r.at[s], (me_b, w))
-        copy.start()
-        sends1.append(copy)
+    each(rows - 1, lambda i: pl.semaphore_signal(
+        barrier, inc=1, device_id=ahead(rows - 1 - i), device_id_type=MESH
+    ))
+    gath[0:1, :] = q_ref[...]
+    pl.semaphore_wait(barrier, rows - 1)
+    each(rows - 1, lambda i: gather_copy(i).start())
 
     def prepare(load, raw, high, low):
         load.wait()
@@ -101,20 +119,9 @@
             low[:patches, g * LANES:(g + 1) * LANES] = l
 
     prepare(k_load, k_in, khi, klo)
-
-    for copy in sends1:
-        copy.wait_recv()
-    own = gath.at[pl.ds(pl.multiple_of(me_b * nwide, nwide), nwide)]
-    sends2 = []
-    for s, b in enumerate(blk_peers):
-        copy = remote(own, own, g2s.at[s], g2r.at[s], (b, me_w))
-        copy.start()
-        sends2.append(copy)
-
     prepare(v_load, v_in, vhi, vlo)
-
-    for copy in sends2:
-        copy.wait_recv()
+    each(rows - 1, lambda i: gather_copy(i).wait_send())
+    each(rows - 1, lambda i: gather_copy(i).wait_recv())
 
     stacked = per_group * block
     row = lax.broadcasted_iota(jnp.int32, (stacked, GROUP), 0) // block
@@ -134,11 +141,13 @@
 
     def chunk(at):
         q = gath[pl.ds(at, block), :]
-        pos = pos_ref[at // block]
-        eye = lax.broadcasted_iota(jnp.int32, (block, block), 0) == lax.broadcasted_iota(
-            jnp.int32, (block, block), 1
+        slot = at + lax.broadcasted_iota(jnp.int32, (block, 1), 0)
+        a, b = offsets(slot, nblk, nwide)
+        caption = (me_b + nblk - a) % nblk * nwide + (me_w + nwide - b) % nwide
+        lane = lax.broadcasted_iota(jnp.int32, (block, rows), 1)
+        label = jnp.sum(
+            jnp.where(lane == caption, pos_ref[...].astype(F32), 0.0), axis=1, keepdims=True
         )
-        label = jnp.sum(jnp.where(eye, pos.astype(F32), 0.0), axis=1, keepdims=True)
         sign = 2.0 * label - 1.0
         q_mean = jnp.mean(q * q, axis=1, keepdims=True)
         qg = [q[:, j * GROUP:(j + 1) * GROUP] for j in range(groups)]
@@ -207,45 +216,26 @@
 
         lax.fori_loop(0, rows // block, step, 0)
 
-    sends3 = []
-    for s, b in enumerate(blk_peers):
-        copy = remote(
-            part.at[pl.ds(pl.multiple_of(b * nwide, nwide), nwide)],
-            land1.at[s], r1s.at[s], r1r.at[s], (b, me_w),
-        )
-        copy.start()
-        sends3.append(copy)
+    each(rows - 1, lambda i: scatter_copy(i).start())
+    own = pltpu.make_async_copy(part.at[0:1], land.at[0:1], store_sem.at[0])
+    own.start()
 
     if one:
         finish(state, False)
-    dk_store = pltpu.make_async_copy(dk_buf, dk_hbm, store_sem.at[0])
-    dv_store = pltpu.make_async_copy(dv_buf, dv_hbm, store_sem.at[1])
-    dk_store.start()
-    dv_store.start()
-
-    total = part[pl.ds(pl.multiple_of(me_b * nwide, nwide), nwide), :]
-    for s, copy in enumerate(sends3):
-        copy.wait_recv()
-        total = total + land1[s]
-    acc[...] = total
-
-    sends4 = []
-    for s, w in enumerate(wide_peers):
-        copy = remote(
-            acc.at[pl.ds(w, 1)], land2.at[pl.ds(s, 1)], r2s.at[s], r2r.at[s], (me_b, w)
-        )
-        copy.start()
-        sends4.append(copy)
-    final = acc[pl.ds(me_w, 1), :]
-    for copy in sends4:
-        copy.wait_recv()
-    final = final + jnp.sum(land2[:nwide - 1, :], axis=0, keepdims=True)
-    dq_ref[...] = final
-
-    for copy in sends1 + sends2 + sends3 + sends4:
-        copy.wait_send()
-    dk_store.wait()
-    dv_store.wait()
+
+    own.wait()
+    each(rows - 1, lambda i: scatter_copy(i).wait_send())
+    each(rows - 1, lambda i: scatter_copy(i).wait_recv())
+
+
+def write_kernel(dk_in, dv_in, land, dk_out, dv_out, dq_ref, sems):
+    dk_copy = pltpu.make_async_copy(dk_in, dk_out, sems.at[0])
+    dv_copy = pltpu.make_async_copy(dv_in, dv_out, sems.at[1])
+    dk_copy.start()
+    dv_copy.start()
+    dq_ref[...] = jnp.sum(land[...], axis=0, keepdims=True)
+    dk_copy.wait()
+    dv_copy.wait()
 
 
 def per_device(nblk, nwide, patch_keys, patch_values, caption_queries, positive):
@@ -253,20 +243,17 @@
     rows = positive.shape[1]
     padded = -(-patches // LANES) * LANES
     block = 32 if rows % 32 == 0 else rows
-    lines = patches * width // LANES
-    flat = (lines, LANES)
-    any_space = pl.BlockSpec(memory_space=pltpu.HBM)
+    flat = (patches * width // LANES, LANES)
+    hbm = pl.BlockSpec(memory_space=pltpu.HBM)
+    anywhere = pl.BlockSpec(memory_space=pl.ANY)
     vmem = pl.BlockSpec(memory_space=pltpu.VMEM)
     dma = pltpu.SemaphoreType.DMA
-    dk, dv, dq = pl.pallas_call(
+    big = jax.ShapeDtypeStruct(flat, F32)
+    dk, dv, land = pl.pallas_call(
         functools.partial(kernel, nblk, nwide, block),
-        out_shape=(
-            jax.ShapeDtypeStruct(flat, F32),
-            jax.ShapeDtypeStruct(flat, F32),
-            jax.ShapeDtypeStruct(caption_queries.shape, F32),
-        ),
-        in_specs=[any_space, any_space, vmem, vmem],
-        out_specs=(any_space, any_space, vmem),
+        out_shape=(pltpu.VMEM(flat, F32), pltpu.VMEM(flat, F32), pltpu.VMEM((rows, width), F32)),
+        in_specs=[hbm, hbm, vmem, vmem],
+        out_specs=(vmem, vmem, vmem),
         scratch_shapes=[
             pltpu.VMEM(flat, F32),
             pltpu.VMEM(flat, F32),
@@ -274,19 +261,11 @@
             pltpu.VMEM((padded, width), BF16),
             pltpu.VMEM((padded, width), BF16),
             pltpu.VMEM((padded, width), BF16),
-            pltpu.VMEM(flat, F32),
-            pltpu.VMEM(flat, F32),
             pltpu.VMEM((rows, width), F32),
             pltpu.VMEM((rows, width), F32),
-            pltpu.VMEM((nblk - 1, nwide, width), F32),
-            pltpu.VMEM((nwide, width), F32),
-            pltpu.VMEM((nwide, width), F32),
             dma((2,)),
-            dma((2,)),
-            dma((nwide - 1,)), dma((nwide - 1,)),
-            dma((nblk - 1,)), dma((nblk - 1,)),
-            dma((nblk - 1,)), dma((nblk - 1,)),
-            dma((nwide - 1,)), dma((nwide - 1,)),
+            dma((1,)),
+            dma((rows - 1,)), dma((rows - 1,)), dma((rows - 1,)), dma((rows - 1,)),
         ],
         compiler_params=pltpu.CompilerParams(
             collective_id=0, has_side_effects=True, vmem_limit_bytes=60 * 1024 * 1024
@@ -300,8 +279,16 @@
         patch_keys.reshape(flat),
         patch_values.reshape(flat),
         caption_queries,
-        positive.reshape(rows // block, 1, block),
+        positive,
     )
+    dk, dv, dq = pl.pallas_call(
+        write_kernel,
+        out_shape=(big, big, jax.ShapeDtypeStruct(caption_queries.shape, F32)),
+        in_specs=[vmem, vmem, vmem],
+        out_specs=(hbm, hbm, vmem),
+        scratch_shapes=[dma((2,))],
+        compiler_params=pltpu.CompilerParams(vmem_limit_bytes=4 * 1024 * 1024),
+    )(dk, dv, land)
     return dk.reshape(patch_keys.shape), dv.reshape(patch_values.shape), dq
 
 

time: 27.5 us -> 23 us (0.84)
  local copies, waits for them, and re-layouts: 3.41 us -> 0 us
  Pallas kernels: 23.3 us -> 22.2 us
    unnamed x7 -> x0, local copies, waits for them, and re-layouts: 3.41 us -> none
    pallas_call x1, Pallas kernels: 23.3 us -> 20.7 us  [per_device(): pl.pallas_call(functools.partial(kernel, nblk, nwide, block), out_shape=(...]
    pallas_call x0 -> x1, Pallas kernels: none -> 1.48 us  [per_device(): pl.pallas_call(write_kernel, out_shape=(big, big, jax.ShapeDtypeStruct(ca...]
where the time goes in v2:
time: 23 us; the launch traced here: 22.8 us
  Pallas kernels  22.2 us (97%)
  between operations  0.64 us (3%)
    pallas_call x1, Pallas kernels, per_device(): pl.pallas_call(functools.partial(kernel, nblk, nwide, block), out_shape=(...  20.7 us
    pallas_call x1, Pallas kernels, per_device(): pl.pallas_call(write_kernel, out_shape=(big, big, jax.ShapeDtypeStruct(ca...  1.48 us

profile of v2, /device:TPU:0, one launch (start us, length us, event | category | flops | bytes accessed | tf_op | source)
XLA Modules:
  0.0 22.8 jit_solution(4860958191690762254)
XLA Ops:
  0.6 20.7 %shard_map.67 = (f32[784,128]{1,0:T(8,128)S(1)}, f32[784,128]{1,0:T(8,128)S(1)}, f32[32,512]{1,0:T(8,128)S(1)}) custom-call(f32[784,128]{1,0:T(8,128)} %bitcast.4, f32[784,128]{1,0:T(8,128)} %bitcast.5, f32[1,512]{1,0:T(1,128)} %q_ref.1, s32[1,32]{1,0:T(1,128)} %pos_ref.1), custom_call_target="tpu_custom_call" | custom-call | flops 115605504 | bytes 1605632 | tf_op jit(solution)/shard_map/pallas_call | solution.py:252
  21.4 1.5 %shard_map.68 = (f32[784,128]{1,0:T(8,128)}, f32[784,128]{1,0:T(8,128)}, f32[1,512]{1,0:T(1,128)}) custom-call(f32[784,128]{1,0:T(8,128)S(1)} %get-tuple-element.9.dk_in, f32[784,128]{1,0:T(8,128)S(1)} %get-tuple-element.10.dv_in, f32[32,512]{1,0:T(8,128)S(1)} %get-tuple-element.11.land), custom_call_target="tpu_custom_call" | custom-call | tf_op jit(solution)/shard_map/pallas_call | solution.py:284

commit v3 on v2

--- a/solution.py
+++ b/solution.py
@@ -33,7 +33,6 @@
 
 
 NN = ((1,), (0,))
-NT = ((1,), (1,))
 TN = ((0,), (0,))
 
 
@@ -56,7 +55,7 @@
     nblk, nwide, block,
     k_hbm, v_hbm, q_ref, pos_ref,
     dk_buf, dv_buf, land,
-    k_in, v_in, khi, klo, vhi, vlo, gath, part,
+    k_in, v_in, khi, klo, vhi, vlo, kht, klt, vht, vlt, gath, part,
     load_sem, store_sem, gs, gr, rs_sem, rr,
 ):
     padded, width = khi.shape
@@ -107,7 +106,7 @@
     pl.semaphore_wait(barrier, rows - 1)
     each(rows - 1, lambda i: gather_copy(i).start())
 
-    def prepare(load, raw, high, low):
+    def prepare(load, raw, high, low, high_t, low_t):
         load.wait()
         if padded > patches:
             tail = patches // 16 * 16
@@ -117,9 +116,13 @@
             h, l = split(raw[pl.ds(g, patches, stride=pieces), :])
             high[:patches, g * LANES:(g + 1) * LANES] = h
             low[:patches, g * LANES:(g + 1) * LANES] = l
-
-    prepare(k_load, k_in, khi, klo)
-    prepare(v_load, v_in, vhi, vlo)
+        for j in range(groups):
+            at = slice(j * GROUP, (j + 1) * GROUP)
+            high_t[at, :] = high[:, at].T
+            low_t[at, :] = low[:, at].T
+
+    prepare(k_load, k_in, khi, klo, kht, klt)
+    prepare(v_load, v_in, vhi, vlo, vht, vlt)
     each(rows - 1, lambda i: gather_copy(i).wait_send())
     each(rows - 1, lambda i: gather_copy(i).wait_recv())
 
@@ -138,6 +141,9 @@
 
     def cut(ref, j):
         return ref[:, j * GROUP:(j + 1) * GROUP]
+
+    def cut_t(ref, j):
+        return ref[j * GROUP:(j + 1) * GROUP, :]
 
     def chunk(at):
         q = gath[pl.ds(at, block), :]
@@ -155,7 +161,7 @@
 
         e, e2, rinv, pooled = [], [], [], []
         for j in range(groups):
-            s = dot3(qbd[j], (cut(khi, j), cut(klo, j)), NT)
+            s = dot3(qbd[j], (cut_t(kht, j), cut_t(klt, j)), NN)
             s = jnp.where(valid, s, -3e38)
             x = jnp.exp(s - jnp.max(s, axis=1, keepdims=True))
             e.append(x)
@@ -181,7 +187,7 @@
             pd = jnp.concatenate([pooled[j]] * per_group, axis=0)
             rs = jnp.sum(full * pd, axis=1, keepdims=True)
             dpbd.append(split(full))
-            dw = dot3(dpbd[j], (cut(vhi, j), cut(vlo, j)), NT)
+            dw = dot3(dpbd[j], (cut_t(vht, j), cut_t(vlt, j)), NN)
             ds = e[j] * (dw - rs)
             ds2.append(split(ds))
             dq = gathered(dot3(ds2[j], (cut(khi, j), cut(klo, j)), NN)) * scale
@@ -261,6 +267,10 @@
             pltpu.VMEM((padded, width), BF16),
             pltpu.VMEM((padded, width), BF16),
             pltpu.VMEM((padded, width), BF16),
+            pltpu.VMEM((width, padded), BF16),
+            pltpu.VMEM((width, padded), BF16),
+            pltpu.VMEM((width, padded), BF16),
+            pltpu.VMEM((width, padded), BF16),
             pltpu.VMEM((rows, width), F32),
             pltpu.VMEM((rows, width), F32),
             dma((2,)),

time: 23 us -> 22.1 us (0.961)
  Pallas kernels: 22.2 us -> 21.3 us
    pallas_call x1, Pallas kernels: 20.7 us -> 19.9 us  [per_device(): pl.pallas_call(functools.partial(kernel, nblk, nwide, block), out_shape=(...]
where the time goes in v3:
time: 22.1 us; the launch traced here: 22 us
  Pallas kernels  21.3 us (96%)
  between operations  0.64 us (3%)
    pallas_call x1, Pallas kernels, per_device(): pl.pallas_call(functools.partial(kernel, nblk, nwide, block), out_shape=(...  19.9 us
    pallas_call x1, Pallas kernels, per_device(): pl.pallas_call(write_kernel, out_shape=(big, big, jax.ShapeDtypeStruct(ca...  1.48 us

profile of v3, /device:TPU:0, one launch (start us, length us, event | category | flops | bytes accessed | tf_op | source)
XLA Modules:
  0.0 22.0 jit_solution(15800861461812665879)
XLA Ops:
  0.6 19.9 %shard_map.67 = (f32[784,128]{1,0:T(8,128)S(1)}, f32[784,128]{1,0:T(8,128)S(1)}, f32[32,512]{1,0:T(8,128)S(1)}) custom-call(f32[784,128]{1,0:T(8,128)} %bitcast.4, f32[784,128]{1,0:T(8,128)} %bitcast.5, f32[1,512]{1,0:T(1,128)} %q_ref.1, s32[1,32]{1,0:T(1,128)} %pos_ref.1), custom_call_target="tpu_custom_call" | custom-call | flops 115605504 | bytes 1605632 | tf_op jit(solution)/shard_map/pallas_call | solution.py:258
  20.5 1.5 %shard_map.68 = (f32[784,128]{1,0:T(8,128)}, f32[784,128]{1,0:T(8,128)}, f32[1,512]{1,0:T(1,128)}) custom-call(f32[784,128]{1,0:T(8,128)S(1)} %get-tuple-element.9.dk_in, f32[784,128]{1,0:T(8,128)S(1)} %get-tuple-element.10.dv_in, f32[32,512]{1,0:T(8,128)S(1)} %get-tuple-element.11.land), custom_call_target="tpu_custom_call" | custom-call | tf_op jit(solution)/shard_map/pallas_call | solution.py:294

commit v4 on v3

--- a/solution.py
+++ b/solution.py
@@ -29,7 +29,11 @@
     def one(x, y):
         return lax.dot_general(x, y, (dims, ((), ())), preferred_element_type=F32)
 
-    return one(a[0], b[0]) + (one(a[0], b[1]) + one(a[1], b[0]))
+    if dims == TN:
+        return one(a[0], b[0]) + (one(a[0], b[1]) + one(a[1], b[0]))
+    m = a[0].shape[0]
+    both = one(jnp.concatenate(a, axis=0), b[0])
+    return both[:m] + (both[m:] + one(a[0], b[1]))
 
 
 NN = ((1,), (0,))
@@ -123,8 +127,6 @@
 
     prepare(k_load, k_in, khi, klo, kht, klt)
     prepare(v_load, v_in, vhi, vlo, vht, vlt)
-    each(rows - 1, lambda i: gather_copy(i).wait_send())
-    each(rows - 1, lambda i: gather_copy(i).wait_recv())
 
     stacked = per_group * block
     row = lax.broadcasted_iota(jnp.int32, (stacked, GROUP), 0) // block
@@ -208,6 +210,9 @@
                 else:
                     dk_buf[lines, :] = dk[:, lanes]
                     dv_buf[lines, :] = dv[:, lanes]
+
+    each(rows - 1, lambda i: gather_copy(i).wait_send())
+    each(rows - 1, lambda i: gather_copy(i).wait_recv())
 
     one = rows == block
     if one:

time: 22.1 us -> 22.1 us (level)
  no operation moved by 1% of the time
where the time goes in v4:
time: 22.1 us; the launch traced here: 22 us
  Pallas kernels  21.3 us (96%)
  between operations  0.64 us (3%)
    pallas_call x1, Pallas kernels, per_device(): pl.pallas_call(functools.partial(kernel, nblk, nwide, block), out_shape=(...  19.8 us
    pallas_call x1, Pallas kernels, per_device(): pl.pallas_call(write_kernel, out_shape=(big, big, jax.ShapeDtypeStruct(ca...  1.48 us

profile of v4, /device:TPU:0, one launch (start us, length us, event | category | flops | bytes accessed | tf_op | source)
XLA Modules:
  0.0 22.0 jit_solution(16327083619615003021)
XLA Ops:
  0.6 19.8 %shard_map.67 = (f32[784,128]{1,0:T(8,128)S(1)}, f32[784,128]{1,0:T(8,128)S(1)}, f32[32,512]{1,0:T(8,128)S(1)}) custom-call(f32[784,128]{1,0:T(8,128)} %bitcast.4, f32[784,128]{1,0:T(8,128)} %bitcast.5, f32[1,512]{1,0:T(1,128)} %q_ref.1, s32[1,32]{1,0:T(1,128)} %pos_ref.1), custom_call_target="tpu_custom_call" | custom-call | flops 115605504 | bytes 1605632 | tf_op jit(solution)/shard_map/pallas_call | solution.py:263
  20.5 1.5 %shard_map.68 = (f32[784,128]{1,0:T(8,128)}, f32[784,128]{1,0:T(8,128)}, f32[1,512]{1,0:T(1,128)}) custom-call(f32[784,128]{1,0:T(8,128)S(1)} %get-tuple-element.9.dk_in, f32[784,128]{1,0:T(8,128)S(1)} %get-tuple-element.10.dv_in, f32[32,512]{1,0:T(8,128)S(1)} %get-tuple-element.11.land), custom_call_target="tpu_custom_call" | custom-call | tf_op jit(solution)/shard_map/pallas_call | solution.py:299
